TPU v7x, 32 devices: a whole 2x2x4 slice. The times are simulated.
32 devices in a mesh: groups: 2 (over x), expert: 16 (over z, y, core), dp: 1.
Axes of the slice: x: 2, y: 2, z: 4, core: 2. Of those that a mesh axis runs over, the one named last changes fastest.
Arguments:
- token_codes: bfloat16 [2048, 4096], P(('groups', 'expert', 'dp')), parts along dimension 0, may hold values from -6 to 6
- token_scales: bfloat16 [2048, 32], P(('groups', 'expert', 'dp')), parts along dimension 0, may hold values from 0.25 to 4
- expert_ids: int32 [2048, 8], P(('groups', 'expert', 'dp')), parts along dimension 0, may hold values from 0 to 15, all different within a row; in each aligned block of 64 rows (0 to 63, 64 to 127, ...) at most 48 rows name the same one
- gate_values: float32 [2048, 8], P(('groups', 'expert', 'dp')), parts along dimension 0, may hold values from 0.05 to 0.25
- w_gate: bfloat16 [16, 4096, 1536], P('expert', None, 'dp'), may hold values from -0.09375 to 0.09375
- w_up: bfloat16 [16, 4096, 1536], P('expert', None, 'dp'), may hold values from -0.09375 to 0.09375
- w_down: bfloat16 [16, 1536, 4096], P('expert', 'dp'), may hold values from -0.15625 to 0.15625
- gate_scales: float32 [16, 32, 12], P('expert', None, 'dp'), may hold values from 0.5 to 2
- up_scales: float32 [16, 32, 12], P('expert', None, 'dp'), may hold values from 0.5 to 2
- down_scales: float32 [16, 12, 32], P('expert', 'dp'), may hold values from 0.5 to 2
Outputs:
- mixed: bfloat16 [2048, 4096], P(('groups', 'expert', 'dp')), parts along dimension 0
There are 2 independent parts, one for each index of `groups`. A program takes and returns all parts, laid end to end along the dimension named above; an argument that names none is the same for every part. Nothing has to cross between parts.
Inputs may be any that keep to these rules, and one draw needn't show every extreme that they name: `expert_ids`: each token names 8 different experts. Among the 64 tokens of one device no expert is named by more than 48 tokens, and in every draw some device names some expert in exactly 48 tokens.
All inputs are finite; a program needn't handle non-finite values.
Results may differ from a plain program's by a relative error of at most 0.028.
Values may be sent and summed in bfloat16 or wider, within the bound.
No kernel may reach another device: no remote copies, remote signals or barrier semaphores. Data moves between devices by JAX's collectives and lax.ppermute only.
A program may use at most 320 MiB of HBM per device.

v0:
```python
import jax
import jax.numpy as jnp
from jax import lax
from jax.sharding import PartitionSpec as P


def dequant_rows(codes, scales):
    count = codes.shape[0]
    blocks = (
        codes.astype(jnp.float32).reshape(count, scales.shape[1], 128)
        * scales.astype(jnp.float32)[:, :, None]
    )
    return blocks.reshape(count, codes.shape[1]).astype(jnp.bfloat16)


def dequant_weight(weight, scales):
    height, breadth = weight.shape
    tiles = (
        weight.astype(jnp.float32).reshape(height // 128, 128, breadth // 128, 128)
        * scales[:, None, :, None]
    )
    return tiles.reshape(height, breadth).astype(jnp.bfloat16)


def swiglu_rows(rows, gate_mat, up_mat, down_mat):
    gated = jnp.dot(rows, gate_mat, preferred_element_type=jnp.float32)
    upward = jnp.dot(rows, up_mat, preferred_element_type=jnp.float32)
    hidden = (jax.nn.silu(gated) * upward).astype(jnp.bfloat16)
    return jnp.dot(hidden, down_mat, preferred_element_type=jnp.float32)


def shards(
    token_codes,
    token_scales,
    expert_ids,
    gate_values,
    w_gate,
    w_up,
    w_down,
    gate_scales,
    up_scales,
    down_scales,
):
    tok_rows, width = token_codes.shape
    top_count = expert_ids.shape[1]
    blocks_wide = token_scales.shape[1]
    peers = lax.axis_size("expert")
    pairs = lax.axis_size("dp")
    capacity = min(tok_rows, 3 * tok_rows * top_count // (2 * peers))
    flat_ids = expert_ids.reshape(-1)
    onehot = (flat_ids[:, None] == jnp.arange(peers, dtype=jnp.int32)[None, :]).astype(jnp.int32)
    earlier = jnp.cumsum(onehot, axis=0) - onehot
    slots = jnp.sum(earlier * onehot, axis=1)
    target = flat_ids * capacity + slots
    source = jnp.arange(tok_rows * top_count, dtype=jnp.int32) // top_count
    send_codes = (
        jnp.zeros((peers * capacity, width), jnp.bfloat16).at[target].set(token_codes[source])
    )
    send_scales = (
        jnp.zeros((peers * capacity, blocks_wide), jnp.bfloat16)
        .at[target]
        .set(token_scales[source])
    )
    send_codes = send_codes.reshape(1, peers, capacity, width)
    send_scales = send_scales.reshape(1, peers, capacity, blocks_wide)
    paired = (
        lax.all_gather(send_codes, "dp", axis=0, tiled=True),
        lax.all_gather(send_scales, "dp", axis=0, tiled=True),
    )
    got_codes, got_scales = (
        lax.all_to_all(paired[0], "expert", split_axis=1, concat_axis=1, tiled=True),
        lax.all_to_all(paired[1], "expert", split_axis=1, concat_axis=1, tiled=True),
    )
    rows = dequant_rows(got_codes.reshape(-1, width), got_scales.reshape(-1, blocks_wide))
    gate_mat = dequant_weight(w_gate[0], gate_scales[0])
    up_mat = dequant_weight(w_up[0], up_scales[0])
    down_mat = dequant_weight(w_down[0], down_scales[0])
    partial_value = swiglu_rows(rows, gate_mat, up_mat, down_mat).reshape(
        pairs, peers * capacity, width
    )
    mine = lax.psum_scatter(
        partial_value.astype(jnp.bfloat16), "dp", scatter_dimension=0, tiled=True
    ).astype(jnp.float32)[0]
    results = mine.astype(jnp.bfloat16).reshape(peers, capacity, width)
    returned = lax.all_to_all(results, "expert", split_axis=0, concat_axis=0, tiled=True).reshape(
        peers * capacity, width
    )
    picked = returned[target].reshape(tok_rows, top_count, width)
    mixed = jnp.sum(picked.astype(jnp.float32) * gate_values[:, :, None], axis=1)
    return mixed.astype(jnp.bfloat16)


def solution(mesh):
    return jax.shard_map(
        shards,
        mesh=mesh,
        in_specs=(
            P(("groups", "expert", "dp"), None),
            P(("groups", "expert", "dp"), None),
            P(("groups", "expert", "dp"), None),
            P(("groups", "expert", "dp"), None),
            P("expert", None, "dp"),
            P("expert", None, "dp"),
            P("expert", "dp", None),
            P("expert", None, "dp"),
            P("expert", None, "dp"),
            P("expert", "dp", None),
        ),
        out_specs=P(("groups", "expert", "dp"), None),
        check_vma=False,
    )
```

profile of v0, /device:TPU:13, one launch (start us, length us, event | category | flops | bytes accessed | tf_op | source)
XLA Modules:
  0.0 421.3 jit_solution(11865154015904351168)
XLA Ops:
  0.0 0.8 copy.43
  0.8 0.1 eq.29
  0.9 0.1 eq.25
  1.0 0.7 broadcast_multiply_fusion
  1.7 1.2 reduce-window.6
  2.9 0.2 slice_reduce_fusion
  3.1 0.1 copy.42
  3.2 0.1 mul.105
  3.3 0.8 copy.46
  4.1 0.1 fusion.31
  4.2 0.0 copy-start.2
  4.2 3.0 scatter_custom_fusion.1
  7.3 0.1 copy.48
  7.4 0.8 reshape.262
  8.3 6.7 %all-to-all-start.1 = ((bf16[16,2,768]{2,1,0:T(2,128)(2,1)}), bf16[16,2,768]{2,1,0:T(2,128)(2,1)S(1)}, u32[]{:S(2)}, u32[]{:S(2)}) async-start(bf16[16,2,768]{2,1,0:T(2,128)(2,1)} %reshape.262), calls=%async_computation.1 | async-start | bytes 98304 | tf_op jit(solution)/shard_map/all_to_all | solution.py:72
  15.0 0.0 copy-done
  15.0 22.2 %scatter_custom_fusion = bf16[768,4096]{1,0:T(8,128)(2,1)} fusion(s32[512]{0:T(512)S(1)} %bitcast.125, bf16[64,4096]{1,0:T(8,128)(2,1)S(1)} %copy-done, s32[1024]{0:T(1024)S(1)} %pad_clamp_fusion.1, bf16[]{:T(256)} %constant.27.clone.1), kind=kCustom, calls=%fused_computation.27 | custom fusion | bytes 6291458 | tf_op jit(solution)/shard_map/scatter | solution.py:57
  37.1 0.0 all-to-all-done.1
  37.2 6.4 %all-to-all-start = ((bf16[1,16,48,4096]{3,2,0,1:T(8,128)(2,1)}), bf16[1,16,48,4096]{3,2,0,1:T(8,128)(2,1)}, u32[]{:S(2)}, u32[]{:S(2)}) async-start(bf16[1,16,48,4096]{3,2,0,1:T(8,128)(2,1)} %bitcast.111), calls=%async_computation | async-start | bytes 12582912 | tf_op jit(solution)/shard_map/all_to_all | solution.py:71
  43.6 17.8 %copy.51 = f32[1,4096,1536]{1,2,0:T(8,128)} copy(bf16[1,4096,1536]{2,1,0:T(8,128)(2,1)} %param.14) | data formatting | bytes 37748736 | tf_op jit(solution)/shard_map/convert_element_type | solution.py:19
  61.4 20.9 %copy.64 = f32[192,8,32,128]{3,2,1,0:T(8,128)} copy(f32[192,8,32,128]{3,1,2,0:T(8,128)} %bitcast.108) | data formatting | bytes 50331648
  82.3 17.8 %copy.52 = f32[1,4096,1536]{1,2,0:T(8,128)} copy(bf16[1,4096,1536]{2,1,0:T(8,128)(2,1)} %param.15) | data formatting | bytes 37748736 | tf_op jit(solution)/shard_map/convert_element_type | solution.py:19
  100.1 0.0 slice-start.2
  100.1 0.0 slice-start.3
  100.1 0.0 slice-start.4
  100.1 0.0 slice-start.5
  100.1 23.2 %copy.66 = f32[192,8,32,128]{3,2,1,0:T(8,128)} copy(f32[192,8,32,128]{3,1,2,0:T(8,128)} %bitcast.109) | data formatting | bytes 50331648
  123.3 0.0 copy-done.5
  123.4 1.0 slice-done.5
  124.4 6.4 %multiply_convert_fusion.1 = bf16[32,128,12,128]{1,0,3,2:T(8,128)(2,1)} fusion(f32[32,128,12,128]{1,0,3,2:T(8,128)S(1)} %bitcast.106, f32[32,12]{0,1:T(8,128)S(1)} %bitcast.122), kind=kLoop, calls=%fused_computation.8 | loop fusion | flops 12582912 | bytes 37750272 | tf_op jit(solution)/shard_map/convert_element_type | solution.py:22
  130.8 14.0 %multiply_convert_fusion = bf16[32,128,12,128]{1,0,3,2:T(8,128)(2,1)} fusion(f32[32,128,12,128]{1,0,3,2:T(8,128)} %bitcast.107, f32[32,12]{0,1:T(8,128)S(1)} %bitcast.123), kind=kLoop, calls=%fused_computation.7 | loop fusion | flops 12582912 | bytes 37750272 | tf_op jit(solution)/shard_map/convert_element_type | solution.py:22
  144.8 0.2 reshape.263
  145.0 0.1 copy.56
  145.1 35.7 %all-to-all-done = bf16[1,16,48,4096]{3,2,0,1:T(8,128)(2,1)} async-done(((bf16[1,16,48,4096]{3,2,0,1:T(8,128)(2,1)}), bf16[1,16,48,4096]{3,2,0,1:T(8,128)(2,1)}, u32[]{:S(2)}, u32[]{:S(2)}) %all-to-all-start) | async-done | bytes 6291488 | tf_op jit(solution)/shard_map/all_to_all | solution.py:71
  180.8 4.9 %copy.62 = f32[96,8,32,128]{3,2,1,0:T(8,128)S(1)} copy(bf16[96,8,32,128]{3,1,2,0:T(8,128)(2,1)} %bitcast.96) | data formatting | bytes 18874368
  185.7 4.1 fusion.9
  189.8 16.9 %fusion.6 = f32[768,1536]{1,0:T(8,128)} fusion(bf16[192,8,32,128]{3,2,1,0:T(8,128)(2,1)} %bitcast.112, bf16[96,8,32,128]{3,2,1,0:T(8,128)(2,1)S(1)} %bitcast.115), kind=kOutput, calls=%fused_computation.13 | convolution fusion | flops 9663676416 | bytes 23592960 | tf_op jit(solution)/shard_map/dot_general | solution.py:26
  206.8 17.6 %multiply_convert_fusion.2 = bf16[768,1536]{1,0:T(8,128)(2,1)} fusion(f32[768,1536]{1,0:T(8,128)} %fusion.6, bf16[192,8,32,128]{3,2,1,0:T(8,128)(2,1)} %bitcast.113, bf16[96,8,32,128]{3,2,1,0:T(8,128)(2,1)S(1)} %bitcast.116), kind=kOutput, calls=%fused_computation.26 | convolution fusion | flops 9670754304 | bytes 25952256 | tf_op jit(solution)/shard_map/dot_general | solution.py:27
  224.4 11.6 %mul.118 = f32[12,128,32,128]{3,2,1,0:T(8,128)} broadcast(f32[12,32]{1,0:T(8,128)S(1)} %bitcast.121), dimensions={0,2} | broadcast | bytes 25167360 | tf_op jit(solution)/shard_map/mul | solution.py:19
  236.0 0.0 copy-done.8
  236.0 23.6 %fusion.12 = bf16[768,4096]{1,0:T(8,128)(2,1)} fusion(bf16[768,1536]{1,0:T(8,128)(2,1)S(1)} %copy-done.8, f32[192,8,32,128]{3,2,1,0:T(8,128)} %bitcast.110, bf16[1,1536,4096]{2,1,0:T(8,128)(2,1)} %param.16), kind=kOutput, calls=%fused_computation.21 | convolution fusion | flops 9685696512 | bytes 46399488 | tf_op jit(solution)/shard_map/dot_general | solution.py:29
  259.6 5.4 %all-to-all-start.2 = ((bf16[16,48,4096]{2,1,0:T(8,128)(2,1)}), bf16[16,48,4096]{2,1,0:T(8,128)(2,1)}, u32[]{:S(2)}, u32[]{:S(2)}) async-start(bf16[16,48,4096]{2,1,0:T(8,128)(2,1)} %bitcast.114), calls=%async_computation.2 | async-start | bytes 12582912 | tf_op jit(solution)/shard_map/all_to_all | solution.py:85
  265.0 0.0 copy-done.7
  265.0 0.1 copy.53
  265.1 0.0 copy-done.3
  265.1 137.2 %all-to-all-done.2 = bf16[16,48,4096]{2,1,0:T(8,128)(2,1)} async-done(((bf16[16,48,4096]{2,1,0:T(8,128)(2,1)}), bf16[16,48,4096]{2,1,0:T(8,128)(2,1)}, u32[]{:S(2)}, u32[]{:S(2)}) %all-to-all-start.2) | async-done | bytes 6291488 | tf_op jit(solution)/shard_map/all_to_all | solution.py:85
  402.2 12.3 %gather_fusion = bf16[512,4096]{1,0:T(8,128)(2,1)} fusion(bf16[768,4096]{1,0:T(8,128)(2,1)} %bitcast.9, s32[1024]{0:T(1024)S(1)} %pad_clamp_fusion), kind=kCustom, calls=%fused_computation.2 | custom fusion | bytes 8390656 | tf_op jit(solution)/shard_map/gather | solution.py:88
  414.5 6.5 %fusion.11 = bf16[64,4096]{1,0:T(8,128)(2,1)} fusion(bf16[512,4096]{1,0:T(8,128)(2,1)} %gather_fusion, f32[64,8]{1,0:T(8,128)S(1)} %copy.53), kind=kLoop, calls=%fused_computation.20 | loop fusion | flops 6029312 | bytes 4720640 | tf_op jit(solution)/shard_map/reduce_sum | solution.py:89
  (30 shorter events, 0.1 us)
Async XLA Ops:
  0.0 15.0 %copy-start = (bf16[64,4096]{1,0:T(8,128)(2,1)S(1)}, bf16[64,4096]{1,0:T(8,128)(2,1)}, u32[]{:S(2)}) copy-start(bf16[64,4096]{1,0:T(8,128)(2,1)} %param.10) | copy-start | bytes 1572868
  4.2 32.9 %copy-start.2 = (s32[512,1]{0,1:T(1,128)}, s32[512,1]{0,1:T(1,128)S(1)}, u32[]{:S(2)}) copy-start(s32[512,1]{0,1:T(1,128)S(1)} %compare_select_fusion.1) | copy-start | bytes 6148
  8.3 28.9 %all-to-all-start.1 = ((bf16[16,2,768]{2,1,0:T(2,128)(2,1)}), bf16[16,2,768]{2,1,0:T(2,128)(2,1)S(1)}, u32[]{:S(2)}, u32[]{:S(2)}) async-start(bf16[16,2,768]{2,1,0:T(2,128)(2,1)} %reshape.262), calls=%async_computation.1 | async-start | bytes 98304 | tf_op jit(solution)/shard_map/all_to_all | solution.py:72
  37.2 143.7 %all-to-all-start = ((bf16[1,16,48,4096]{3,2,0,1:T(8,128)(2,1)}), bf16[1,16,48,4096]{3,2,0,1:T(8,128)(2,1)}, u32[]{:S(2)}, u32[]{:S(2)}) async-start(bf16[1,16,48,4096]{3,2,0,1:T(8,128)(2,1)} %bitcast.111), calls=%async_computation | async-start | bytes 12582912 | tf_op jit(solution)/shard_map/all_to_all | solution.py:71
  61.4 20.9 %copy-start.4 = (f32[1,32,12]{1,0,2:T(1,128)S(1)}, f32[1,32,12]{1,0,2:T(1,128)}, u32[]{:S(2)}) copy-start(f32[1,32,12]{1,0,2:T(1,128)} %param.17) | copy-start | bytes 4612
  100.1 23.3 %slice-start = ((s8[25165824]{0:T(1024)(128)(4,1)}), s8[4194304]{0:T(1024)(128)(4,1)S(1)}, s32[]{:S(2)}) async-start(s8[25165824]{0:T(1024)(128)(4,1)} %bitcast.104), calls=%async_computation.3 | async-start | bytes 8388608
  100.1 23.2 %copy-start.5 = (f32[1,32,12]{1,0,2:T(1,128)S(1)}, f32[1,32,12]{1,0,2:T(1,128)}, u32[]{:S(2)}) copy-start(f32[1,32,12]{1,0,2:T(1,128)} %param.18) | copy-start | bytes 4612
  100.1 23.2 %copy-start.6 = (f32[1,12,32]{2,0,1:T(1,128)S(1)}, f32[1,12,32]{2,0,1:T(1,128)}, u32[]{:S(2)}) copy-start(f32[1,12,32]{2,0,1:T(1,128)} %param.19) | copy-start | bytes 4612
  100.1 23.3 %slice-start.1 = ((s8[25165824]{0:T(1024)(128)(4,1)}), s8[4194304]{0:T(1024)(128)(4,1)S(1)}, s32[]{:S(2)}) async-start(s8[25165824]{0:T(1024)(128)(4,1)} %bitcast.104), calls=%async_computation.4 | async-start | bytes 8388608
  100.1 23.3 %slice-start.2 = ((s8[25165824]{0:T(1024)(128)(4,1)}), s8[4194304]{0:T(1024)(128)(4,1)S(1)}, s32[]{:S(2)}) async-start(s8[25165824]{0:T(1024)(128)(4,1)} %bitcast.104), calls=%async_computation.5 | async-start | bytes 8388608
  100.1 23.3 %slice-start.3 = ((s8[25165824]{0:T(1024)(128)(4,1)}), s8[4194304]{0:T(1024)(128)(4,1)S(1)}, s32[]{:S(2)}) async-start(s8[25165824]{0:T(1024)(128)(4,1)} %bitcast.104), calls=%async_computation.6 | async-start | bytes 8388608
  100.1 23.3 %slice-start.4 = ((s8[25165824]{0:T(1024)(128)(4,1)}), s8[4194304]{0:T(1024)(128)(4,1)S(1)}, s32[]{:S(2)}) async-start(s8[25165824]{0:T(1024)(128)(4,1)} %bitcast.104), calls=%async_computation.7 | async-start | bytes 8388608
  100.1 24.3 %slice-start.5 = ((s8[25165824]{0:T(1024)(128)(4,1)}), s8[4194304]{0:T(1024)(128)(4,1)S(1)}, s32[]{:S(2)}) async-start(s8[25165824]{0:T(1024)(128)(4,1)} %bitcast.104), calls=%async_computation.8 | async-start | bytes 8388608
  224.4 11.6 %copy-start.8 = (bf16[768,1536]{1,0:T(8,128)(2,1)S(1)}, bf16[768,1536]{1,0:T(8,128)(2,1)}, u32[]{:S(2)}) copy-start(bf16[768,1536]{1,0:T(8,128)(2,1)} %multiply_convert_fusion.2) | copy-start | bytes 7077892
  259.5 5.4 %copy-start.7 = (f32[64,8]{0,1:T(8,128)S(1)}, f32[64,8]{0,1:T(8,128)}, u32[]{:S(2)}) copy-start(f32[64,8]{0,1:T(8,128)} %param.13) | copy-start | bytes 6148
  259.5 5.5 %copy-start.3 = (s32[512,1]{0,1:T(1,128)S(1)}, s32[512,1]{0,1:T(1,128)}, u32[]{:S(2)}) copy-start(s32[512,1]{0,1:T(1,128)} %copy-done.2) | copy-start | bytes 6148
  259.6 142.7 %all-to-all-start.2 = ((bf16[16,48,4096]{2,1,0:T(8,128)(2,1)}), bf16[16,48,4096]{2,1,0:T(8,128)(2,1)}, u32[]{:S(2)}, u32[]{:S(2)}) async-start(bf16[16,48,4096]{2,1,0:T(8,128)(2,1)} %bitcast.114), calls=%async_computation.2 | async-start | bytes 12582912 | tf_op jit(solution)/shard_map/all_to_all | solution.py:85
  402.2 18.7 %copy-start.1 = (bf16[64,4096]{1,0:T(8,128)(2,1)S(1)}, bf16[64,4096]{1,0:T(8,128)(2,1)}, u32[]{:S(2)}) copy-start(bf16[64,4096]{1,0:T(8,128)(2,1)} %param.10) | copy-start | bytes 1572868
where the time goes:
time: 426 us; the launch traced here: 421 us
  waiting for transfers between devices  173 us (41%)
  local copies, waits for them, and re-layouts  138 us (32%)
  matrix products  58.1 us (14%)
  other arithmetic  33 us (8%)
  starting transfers between devices  18.5 us (4%)
    all_to_all x1, waiting for transfers between devices, shards(): lax.all_to_all(results, 'expert', split_axis=0, concat_axis=0, tiled=True)  137 us
    unnamed x41, local copies, waits for them, and re-layouts  52.7 us
    all_to_all x1, waiting for transfers between devices, shards(): lax.all_to_all(paired[0], 'expert', split_axis=1, concat_axis=1, tiled=True)  35.7 us
    convert_element_type x2, local copies, waits for them, and re-layouts, dequant_weight(): weight.astype(jnp.float32).reshape(height // 128, 128, breadth // 128, 128)  35.6 us
    dot_general x1, matrix products, swiglu_rows(): return jnp.dot(hidden, down_mat, preferred_element_type=jnp.float32)  23.6 us
    scatter x1, local copies, waits for them, and re-layouts, shards(): jnp.zeros((peers * capacity, width), jnp.bfloat16).at[target]  22.2 us
    convert_element_type x2, other arithmetic, dequant_weight(): return tiles.reshape(height, breadth).astype(jnp.bfloat16)  20.4 us
    dot_general x1, matrix products, swiglu_rows(): upward = jnp.dot(rows, up_mat, preferred_element_type=jnp.float32)  17.6 us
  transfers between devices with their start and end apart: 3, of which 2 were waited for; matrix products, arithmetic and copies ran while one was open for 29% of the time, Pallas kernels for 0%

commit v1 on v0

v1 whole, which is shorter than its diff:
```python
import functools

import jax
import jax.numpy as jnp
from jax import lax
from jax.experimental import pallas as pl
from jax.experimental.pallas import tpu as pltpu
from jax.sharding import PartitionSpec as P

BF16 = jnp.bfloat16
F32 = jnp.float32
TILE_FF = 256
TILE_D = 512
MB = 1 << 20


def prep_kernel(codes_ref, scales_ref, ids_ref, gates_ref, first_ref, second_ref, *, experts):
    count, width = codes_ref.shape
    half = count // 2
    scales = scales_ref[...].astype(F32)
    for b in range(width // 128):
        columns = pl.ds(b * 128, 128)
        rows = (codes_ref[:, columns].astype(F32) * scales[:, b : b + 1]).astype(BF16)
        first_ref[:, columns] = rows[:half]
        second_ref[:, columns] = rows[half:]
    lane = lax.broadcasted_iota(jnp.int32, (count, 128), 1)
    expert = lane % experts
    dense = jnp.zeros((count, 128), F32)
    for k in range(ids_ref.shape[1]):
        dense = dense + jnp.where(ids_ref[:, k : k + 1] == expert, gates_ref[:, k : k + 1], 0.0)
    high = dense.astype(BF16).astype(F32)
    both = jnp.where(lane < experts, high, jnp.where(lane < 2 * experts, dense - high, 0.0)).astype(BF16)
    columns = pl.ds(width, 128)
    first_ref[:, columns] = both[:half]
    second_ref[:, columns] = both[half:]


def prep(codes, scales, ids, gates, experts):
    count, width = codes.shape
    shape = jax.ShapeDtypeStruct((count // 2, width + 128), BF16)
    return pl.pallas_call(
        functools.partial(prep_kernel, experts=experts),
        out_shape=(shape, shape),
        cost_estimate=pl.CostEstimate(flops=count * width, bytes_accessed=4 * count * width, transcendentals=0),
        name="prep",
    )(codes, scales, ids, gates)


def dequant_kernel(scales_ref, weight_ref, out_ref, *, tile):
    step = pl.program_id(0)
    height, breadth = weight_ref.shape
    for b in range(height // 128):
        for j in range(breadth // 128):
            scale = scales_ref[step * (height // 128) + b, j]
            block = weight_ref[pl.ds(b * 128, 128), pl.ds(j * 128, 128)].astype(F32) * scale
            out_ref[j * 128 // tile, pl.ds(b * 128, 128), pl.ds(j * 128 % tile, 128)] = block.astype(BF16)


def dequant(weight, scales, tile, name):
    height, breadth = weight.shape
    rows = 256 if breadth > 2048 else 512
    return pl.pallas_call(
        functools.partial(dequant_kernel, tile=tile),
        grid=(height // rows,),
        in_specs=[
            pl.BlockSpec(memory_space=pltpu.SMEM),
            pl.BlockSpec((rows, breadth), lambda i: (i, 0)),
        ],
        out_specs=pl.BlockSpec((breadth // tile, rows, tile), lambda i: (0, i, 0)),
        out_shape=jax.ShapeDtypeStruct((breadth // tile, height, tile), BF16),
        cost_estimate=pl.CostEstimate(flops=height * breadth, bytes_accessed=4 * height * breadth, transcendentals=0),
        compiler_params=pltpu.CompilerParams(vmem_limit_bytes=16 * MB),
        name=name,
    )(scales, weight)


def hidden_kernel(expert_ref, rows_ref, gate_ref, up_ref, hidden_ref, *, experts):
    width = gate_ref.shape[1]
    rows = rows_ref[:, :width]
    gated = jnp.dot(rows, gate_ref[0], preferred_element_type=F32)
    upward = jnp.dot(rows, up_ref[0], preferred_element_type=F32)
    sent = rows_ref[:, width:].astype(F32)
    lane = lax.broadcasted_iota(jnp.int32, sent.shape, 1)
    mine = expert_ref[0]
    value = jnp.sum(jnp.where((lane == mine) | (lane == mine + experts), sent, 0.0), axis=1, keepdims=True)
    hidden_ref[...] = (gated / (1.0 + jnp.exp(-gated)) * upward * value).astype(BF16)


def hidden_of(expert, rows, gate_mat, up_mat, experts):
    count = rows.shape[0]
    tiles, width, tile = gate_mat.shape
    return pl.pallas_call(
        functools.partial(hidden_kernel, experts=experts),
        grid=(tiles,),
        in_specs=[
            pl.BlockSpec(memory_space=pltpu.SMEM),
            pl.BlockSpec(rows.shape, lambda i: (0, 0)),
            pl.BlockSpec((1, width, tile), lambda i: (i, 0, 0)),
            pl.BlockSpec((1, width, tile), lambda i: (i, 0, 0)),
        ],
        out_specs=pl.BlockSpec((count, tile), lambda i: (0, i)),
        out_shape=jax.ShapeDtypeStruct((count, tiles * tile), BF16),
        cost_estimate=pl.CostEstimate(
            flops=4 * count * width * tiles * tile,
            bytes_accessed=4 * width * tiles * tile + 2 * count * width,
            transcendentals=count * tiles * tile,
        ),
        compiler_params=pltpu.CompilerParams(vmem_limit_bytes=40 * MB),
        name="hidden",
    )(expert, rows, gate_mat, up_mat)


def down_kernel(hidden_ref, down_ref, out_ref):
    out_ref[...] = jnp.dot(hidden_ref[...], down_ref[0], preferred_element_type=F32).astype(BF16)


def down_of(hidden, part, down_mat):
    count, depth = hidden.shape
    count //= 2
    tiles, _, tile = down_mat.shape
    return pl.pallas_call(
        down_kernel,
        grid=(tiles,),
        in_specs=[
            pl.BlockSpec((count, depth), lambda i: (part, 0)),
            pl.BlockSpec((1, depth, tile), lambda i: (i, 0, 0)),
        ],
        out_specs=pl.BlockSpec((count, tile), lambda i: (0, i)),
        out_shape=jax.ShapeDtypeStruct((count, tiles * tile), BF16),
        cost_estimate=pl.CostEstimate(
            flops=2 * count * depth * tiles * tile,
            bytes_accessed=2 * depth * tiles * tile + 2 * count * tiles * tile,
            transcendentals=0,
        ),
        compiler_params=pltpu.CompilerParams(vmem_limit_bytes=24 * MB),
        name="down",
    )(hidden, down_mat)


def total_of(*terms):
    return sum(t.astype(F32) for t in terms).astype(BF16)


def solution(mesh):
    experts, pairs = mesh.shape["expert"], mesh.shape["dp"]
    chips = experts * pairs // 2
    if pairs == 1:
        walk = [*range(0, chips, 2), *reversed(range(1, chips, 2))]
    else:
        walk = [*range(chips)]
    far = chips // 2
    names = ("expert", "dp")

    def shift(k):
        return [
            (2 * walk[p] + core, 2 * walk[(p + k) % chips] + core)
            for p in range(chips)
            for core in range(2)
        ]

    def right(a):
        return lax.ppermute(a, names, shift(1))

    def left(a):
        return lax.ppermute(a, names, shift(-1))

    def across(a):
        return lax.ppermute(a, names, [(i, i ^ 1) for i in range(2 * chips)])

    def gather(block):
        half = block.shape[0] // 2
        r = l = block
        own, other, held = [block], [], [block]
        for k in range(1, far):
            r, l = right(r), left(l)
            held += [r, l]
            other.append(across(jnp.concatenate(held)))
            own += [r, l]
            held = []
        last = jnp.concatenate([right(r[:half]), left(l[half:])])
        return jnp.concatenate([*own, last, *other, across(last)]), (r, l)

    def scatter(mine, theirs, block):
        half = block // 2

        def terms(k, side):
            if k == 0:
                at, size = 0, block
            elif k == far:
                at, size = (2 * far - 1) * block + side * half, half
            else:
                at, size = (2 * k - 1 + side) * block, block
            return mine[at : at + size], theirs[at : at + size]

        blank = jnp.zeros((half, mine.shape[1]), BF16)
        r = jnp.concatenate([blank, right(total_of(*terms(far, 1)))])
        l = jnp.concatenate([left(total_of(*terms(far, 0))), blank])
        for k in range(far - 1, 0, -1):
            r = right(total_of(r, *terms(k, 1)))
            l = left(total_of(l, *terms(k, 0)))
        return total_of(r, l, *terms(0, 0))

    def shards(codes, scales, ids, gates, w_gate, w_up, w_down, gate_scales, up_scales, down_scales):
        expert = lax.axis_index("expert").reshape(1)
        first, second = prep(codes, scales, ids, gates, experts)
        block = first.shape[0]
        rows1, seen = gather(first)
        second, _ = lax.optimization_barrier((second, seen))
        rows2, _ = gather(second)
        gate_mat = dequant(w_gate[0], gate_scales[0], TILE_FF, "dequant_gate")
        up_mat = dequant(w_up[0], up_scales[0], TILE_FF, "dequant_up")
        down_mat = dequant(w_down[0], down_scales[0], TILE_D, "dequant_down")
        outs = []
        for rows in (rows1, rows2):
            hidden = hidden_of(expert, rows, gate_mat, up_mat, experts)
            theirs = across(down_of(hidden, 1, down_mat))
            mine = down_of(hidden, 0, down_mat)
            outs.append(scatter(mine, theirs, block))
        return jnp.concatenate(outs)

    token = P(("groups", "expert", "dp"), None)
    return jax.shard_map(
        shards,
        mesh=mesh,
        in_specs=(
            token,
            token,
            token,
            token,
            P("expert", None, "dp"),
            P("expert", None, "dp"),
            P("expert", "dp", None),
            P("expert", None, "dp"),
            P("expert", None, "dp"),
            P("expert", "dp", None),
        ),
        out_specs=token,
        check_vma=False,
    )
```

time: 426 us -> 212 us (0.50)
  the two profiles are of different devices: /device:TPU:13 before, /device:TPU:0 now
where the time goes in v1:
time: 212 us; the launch traced here: 211 us
  Pallas kernels  66.9 us (32%)
  waiting for transfers between devices  60.4 us (28%)
  local copies, waits for them, and re-layouts  44.3 us (21%)
  starting transfers between devices  36.3 us (17%)
  other arithmetic  2.64 us (1%)
    unnamed x54, local copies, waits for them, and re-layouts  43.5 us
    pallas_call x2, Pallas kernels, hidden_of(): pl.pallas_call(functools.partial(hidden_kernel, experts=experts), grid=(t...  33.2 us
    ppermute x16, waiting for transfers between devices, right(): return lax.ppermute(a, names, shift(1))  31.2 us
    ppermute x16, waiting for transfers between devices, left(): return lax.ppermute(a, names, shift(-1))  29.2 us
    ppermute x16, starting transfers between devices, left(): return lax.ppermute(a, names, shift(-1))  25 us
    pallas_call x4, Pallas kernels, down_of(): pl.pallas_call(down_kernel, grid=(tiles,), in_specs=[pl.BlockSpec((count,...  18.8 us
    pallas_call x3, Pallas kernels, dequant(): pl.pallas_call(functools.partial(dequant_kernel, tile=tile), grid=(height...  12.7 us
    ppermute x16, starting transfers between devices, right(): return lax.ppermute(a, names, shift(1))  9.23 us
  transfers between devices with their start and end apart: 42, of which 24 were waited for; matrix products, arithmetic and copies ran while one was open for 8% of the time, Pallas kernels for 31%

profile of v1, /device:TPU:0, one launch (start us, length us, event | category | flops | bytes accessed | tf_op | source)
XLA Modules:
  0.0 211.0 jit_solution(15863988149586522087)
XLA Ops:
  1.4 1.4 copy.12.ids_ref
  2.8 1.4 copy.13.gates_ref
  4.1 2.3 %prep.1 = (bf16[32,4224]{1,0:T(8,128)(2,1)}, bf16[32,4224]{1,0:T(8,128)(2,1)}) custom-call(bf16[64,4096]{1,0:T(8,128)(2,1)} %codes_ref.1, bf16[64,32]{1,0:T(8,128)(2,1)} %copy.11.scales_ref, s32[64,8]{1,0:T(8,128)} %copy.12.ids_ref, f32[64,8]{1,0:T(8,128)} %copy.13.gates_ref), custom_call_target="tpu_custom_call" | custom-call | flops 262144 | bytes 1048576 | tf_op jit(solution)/shard_map/prep/pallas_call | solution.py:41
  6.4 3.0 %collective-permute-start.1 = (bf16[32,4224]{1,0:T(8,128)(2,1)}, bf16[32,4224]{1,0:T(8,128)(2,1)S(1)}, u32[]{:S(2)}, u32[]{:S(2)}) collective-permute-start(bf16[32,4224]{1,0:T(8,128)(2,1)} %get-tuple-element.8), channel_id=1, source_target_pairs={{0,2},{1,3},{4,0},{5,1},{8,4},{9,5},{12,8},{13,9},{14,12},{15,13},... | collective-permute-start | bytes 811016 | tf_op jit(solution)/shard_map/ppermute | solution.py:165
  9.4 1.7 constant_dynamic-update-slice_fusion.12
  13.4 4.6 %copy-done.1 = bf16[1,4096,1536]{2,1,0:T(8,128)(2,1)S(1)} copy-done((bf16[1,4096,1536]{2,1,0:T(8,128)(2,1)S(1)}, bf16[1,4096,1536]{2,1,0:T(8,128)(2,1)}, u32[]{:S(2)}) %copy-start.1) | copy-done | bytes 12582936
  18.0 4.3 %dequant_up.1.up_ref = bf16[6,4096,256]{2,1,0:T(8,128)(2,1)S(1)} custom-call(f32[32,12]{1,0:T(8,128)S(1)} %bitcast.13, bf16[4096,1536]{1,0:T(8,128)(2,1)S(1)} %bitcast.10), custom_call_target="tpu_custom_call" | custom-call | flops 6291456 | bytes 25165824 | tf_op jit(solution)/shard_map/dequant_up/pallas_call | solution.py:62
  22.3 4.5 %copy-done.3 = bf16[6,4096,256]{2,1,0:T(8,128)(2,1)} copy-done((bf16[6,4096,256]{2,1,0:T(8,128)(2,1)}, bf16[6,4096,256]{2,1,0:T(8,128)(2,1)S(1)}, u32[]{:S(2)}) %copy-start.3) | copy-done | bytes 12582936
  26.8 4.3 %dequant_gate.1.gate_ref = bf16[6,4096,256]{2,1,0:T(8,128)(2,1)S(1)} custom-call(f32[32,12]{1,0:T(8,128)S(1)} %bitcast.12, bf16[4096,1536]{1,0:T(8,128)(2,1)S(1)} %bitcast.11), custom_call_target="tpu_custom_call" | custom-call | flops 6291456 | bytes 25165824 | tf_op jit(solution)/shard_map/dequant_gate/pallas_call | solution.py:62
  31.1 4.6 %copy-done.4 = bf16[6,4096,256]{2,1,0:T(8,128)(2,1)} copy-done((bf16[6,4096,256]{2,1,0:T(8,128)(2,1)}, bf16[6,4096,256]{2,1,0:T(8,128)(2,1)S(1)}, u32[]{:S(2)}) %copy-start.4) | copy-done | bytes 12582936
  35.7 4.6 %copy-done = bf16[1,1536,4096]{2,1,0:T(8,128)(2,1)S(1)} copy-done((bf16[1,1536,4096]{2,1,0:T(8,128)(2,1)S(1)}, bf16[1,1536,4096]{2,1,0:T(8,128)(2,1)}, u32[]{:S(2)}) %copy-start) | copy-done | bytes 12582936
  40.3 4.1 %dequant_down.1.down_ref = bf16[8,1536,512]{2,1,0:T(8,128)(2,1)S(1)} custom-call(f32[12,32]{1,0:T(8,128)S(1)} %bitcast.14, bf16[1536,4096]{1,0:T(8,128)(2,1)S(1)} %bitcast.9), custom_call_target="tpu_custom_call" | custom-call | flops 6291456 | bytes 25165824 | tf_op jit(solution)/shard_map/dequant_down/pallas_call | solution.py:62
  44.6 2.0 collective-permute-start.3
  46.8 6.9 %collective-permute-done.3 = bf16[32,4224]{1,0:T(8,128)(2,1)S(1)} collective-permute-done((bf16[32,4224]{1,0:T(8,128)(2,1)S(1)}, bf16[32,4224]{1,0:T(8,128)(2,1)S(1)}, u32[]{:S(2)}, u32[]{:S(2)}) %collective-permute-start.3) | collective-permute-done | bytes 270368 | tf_op jit(solution)/shard_map/ppermute | solution.py:165
  53.7 1.4 collective-permute-done.2
  55.3 1.6 collective-permute-start.5
  57.4 6.7 %collective-permute-done.5 = bf16[32,4224]{1,0:T(8,128)(2,1)S(1)} collective-permute-done((bf16[32,4224]{1,0:T(8,128)(2,1)S(1)}, bf16[32,4224]{1,0:T(8,128)(2,1)S(1)}, u32[]{:S(2)}, u32[]{:S(2)}) %collective-permute-start.5) | collective-permute-done | bytes 270368 | tf_op jit(solution)/shard_map/ppermute | solution.py:165
  65.5 1.6 collective-permute-start.22
  67.8 1.6 collective-permute-start.7
  70.0 6.0 %collective-permute-done.7 = bf16[16,4224]{1,0:T(8,128)(2,1)S(1)} collective-permute-done((bf16[16,4224]{1,0:T(8,128)(2,1)S(1)}, bf16[16,4224]{1,0:T(8,128)(2,1)S(1)}, u32[]{:S(2)}, u32[]{:S(2)}) %collective-permute-start.7) | collective-permute-done | bytes 135200 | tf_op jit(solution)/shard_map/ppermute | solution.py:165
  77.2 5.7 %collective-permute-done.21 = bf16[32,4224]{1,0:T(8,128)(2,1)S(1)} collective-permute-done((bf16[32,4224]{1,0:T(8,128)(2,1)S(1)}, bf16[32,4224]{1,0:T(8,128)(2,1)S(1)}, u32[]{:S(2)}, u32[]{:S(2)}) %collective-permute-start.21) | collective-permute-done | bytes 270368 | tf_op jit(solution)/shard_map/ppermute | solution.py:162
  83.0 1.6 collective-permute-start.24
  86.8 2.0 copy-done.6
  88.8 2.2 %copy-done.7 = bf16[512,4224]{1,0:T(8,128)(2,1)S(1)} copy-done((bf16[512,4224]{1,0:T(8,128)(2,1)S(1)}, bf16[512,4224]{1,0:T(8,128)(2,1)}, u32[]{:S(2)}) %copy-start.7) | copy-done | bytes 4325400
  91.0 16.6 %hidden.2.hidden_ref = bf16[512,1536]{1,0:T(8,128)(2,1)S(1)} custom-call(s32[1]{0:T(128)} %bitcast.expert_ref, bf16[512,4224]{1,0:T(8,128)(2,1)S(1)} %copy-done.7, bf16[6,4096,256]{2,1,0:T(8,128)(2,1)} %copy-done.4, bf16[6,4096,256]{2,1,0:T(8,128)(2,1)} %copy-done.3), custom_call_target="tpu_custom_call" | custom-call | flops 12884901888 | bytes 29360128 | tf_op jit(solution)/shard_map/hidden/pallas_call | solution.py:92
  107.7 4.7 %down.5 = bf16[256,4096]{1,0:T(8,128)(2,1)S(1)} custom-call(bf16[512,1536]{1,0:T(8,128)(2,1)S(1)} %hidden.2.hidden_ref, bf16[8,1536,512]{2,1,0:T(8,128)(2,1)S(1)} %dequant_down.1.down_ref), custom_call_target="tpu_custom_call" | custom-call | flops 3221225472 | bytes 14680064 | tf_op jit(solution)/shard_map/down/pallas_call | solution.py:121
  113.1 1.6 collective-permute-start.26
  116.5 5.0 %collective-permute-done.26 = bf16[32,4224]{1,0:T(8,128)(2,1)S(1)} collective-permute-done((bf16[32,4224]{1,0:T(8,128)(2,1)S(1)}, bf16[32,4224]{1,0:T(8,128)(2,1)S(1)}, u32[]{:S(2)}, u32[]{:S(2)}) %collective-permute-start.26) | collective-permute-done | bytes 270368 | tf_op jit(solution)/shard_map/ppermute | solution.py:165
  121.5 1.6 collective-permute-start.28
  125.2 1.4 collective-permute-done.28
  126.6 1.6 collective-permute-done.27
  129.7 2.1 constant_dynamic-update-slice_fusion.16
  134.3 2.2 %copy-done.5 = bf16[512,4224]{1,0:T(8,128)(2,1)S(1)} copy-done((bf16[512,4224]{1,0:T(8,128)(2,1)S(1)}, bf16[512,4224]{1,0:T(8,128)(2,1)}, u32[]{:S(2)}) %copy-start.5) | copy-done | bytes 4325400
  136.5 16.6 %hidden.3.hidden_ref = bf16[512,1536]{1,0:T(8,128)(2,1)S(1)} custom-call(s32[1]{0:T(128)} %bitcast.expert_ref, bf16[512,4224]{1,0:T(8,128)(2,1)S(1)} %copy-done.5, bf16[6,4096,256]{2,1,0:T(8,128)(2,1)} %copy-done.4, bf16[6,4096,256]{2,1,0:T(8,128)(2,1)} %copy-done.3), custom_call_target="tpu_custom_call" | custom-call | flops 12884901888 | bytes 29360128 | tf_op jit(solution)/shard_map/hidden/pallas_call | solution.py:92
  153.1 4.7 %down.7 = bf16[256,4096]{1,0:T(8,128)(2,1)S(1)} custom-call(bf16[512,1536]{1,0:T(8,128)(2,1)S(1)} %hidden.3.hidden_ref, bf16[8,1536,512]{2,1,0:T(8,128)(2,1)S(1)} %dequant_down.1.down_ref), custom_call_target="tpu_custom_call" | custom-call | flops 3221225472 | bytes 14680064 | tf_op jit(solution)/shard_map/down/pallas_call | solution.py:121
  158.4 4.7 %down.4 = bf16[256,4096]{1,0:T(8,128)(2,1)S(1)} custom-call(bf16[512,1536]{1,0:T(8,128)(2,1)S(1)} %hidden.2.hidden_ref, bf16[8,1536,512]{2,1,0:T(8,128)(2,1)S(1)} %dequant_down.1.down_ref), custom_call_target="tpu_custom_call" | custom-call | flops 3221225472 | bytes 14680064 | tf_op jit(solution)/shard_map/down/pallas_call | solution.py:121
  163.0 4.7 %down.6 = bf16[256,4096]{1,0:T(8,128)(2,1)S(1)} custom-call(bf16[512,1536]{1,0:T(8,128)(2,1)S(1)} %hidden.3.hidden_ref, bf16[8,1536,512]{2,1,0:T(8,128)(2,1)S(1)} %dequant_down.1.down_ref), custom_call_target="tpu_custom_call" | custom-call | flops 3221225472 | bytes 14680064 | tf_op jit(solution)/shard_map/down/pallas_call | solution.py:121
  168.3 1.6 collective-permute-start.17
  170.5 1.6 collective-permute-start.38
  172.1 2.2 %collective-permute-done.13 = bf16[16,4096]{1,0:T(8,128)(2,1)S(1)} collective-permute-done((bf16[16,4096]{1,0:T(8,128)(2,1)S(1)}, bf16[16,4096]{1,0:T(8,128)(2,1)S(1)}, u32[]{:S(2)}, u32[]{:S(2)}) %collective-permute-start.13) | collective-permute-done | bytes 131104 | tf_op jit(solution)/shard_map/ppermute | solution.py:162
  175.4 1.6 collective-permute-start.18
  177.6 1.6 collective-permute-start.39
  179.3 4.9 %collective-permute-done.14 = bf16[32,4096]{1,0:T(8,128)(2,1)S(1)} collective-permute-done((bf16[32,4096]{1,0:T(8,128)(2,1)S(1)}, bf16[32,4096]{1,0:T(8,128)(2,1)S(1)}, u32[]{:S(2)}, u32[]{:S(2)}) %collective-permute-start.14) | collective-permute-done | bytes 262176 | tf_op jit(solution)/shard_map/ppermute | solution.py:162
  186.9 2.9 %collective-permute-done.35 = bf16[32,4096]{1,0:T(8,128)(2,1)S(1)} collective-permute-done((bf16[32,4096]{1,0:T(8,128)(2,1)S(1)}, bf16[32,4096]{1,0:T(8,128)(2,1)S(1)}, u32[]{:S(2)}, u32[]{:S(2)}) %collective-permute-start.35) | collective-permute-done | bytes 262176 | tf_op jit(solution)/shard_map/ppermute | solution.py:162
  192.5 2.9 %collective-permute-done.15 = bf16[32,4096]{1,0:T(8,128)(2,1)S(1)} collective-permute-done((bf16[32,4096]{1,0:T(8,128)(2,1)S(1)}, bf16[32,4096]{1,0:T(8,128)(2,1)S(1)}, u32[]{:S(2)}, u32[]{:S(2)}) %collective-permute-start.15) | collective-permute-done | bytes 262176 | tf_op jit(solution)/shard_map/ppermute | solution.py:162
  198.2 2.9 %collective-permute-done.36 = bf16[32,4096]{1,0:T(8,128)(2,1)S(1)} collective-permute-done((bf16[32,4096]{1,0:T(8,128)(2,1)S(1)}, bf16[32,4096]{1,0:T(8,128)(2,1)S(1)}, u32[]{:S(2)}, u32[]{:S(2)}) %collective-permute-start.36) | collective-permute-done | bytes 262176 | tf_op jit(solution)/shard_map/ppermute | solution.py:162
  203.8 2.9 %collective-permute-done.16 = bf16[32,4096]{1,0:T(8,128)(2,1)S(1)} collective-permute-done((bf16[32,4096]{1,0:T(8,128)(2,1)S(1)}, bf16[32,4096]{1,0:T(8,128)(2,1)S(1)}, u32[]{:S(2)}, u32[]{:S(2)}) %collective-permute-start.16) | collective-permute-done | bytes 262176 | tf_op jit(solution)/shard_map/ppermute | solution.py:162
  207.3 2.6 %collective-permute-done.37 = bf16[32,4096]{1,0:T(8,128)(2,1)S(1)} collective-permute-done((bf16[32,4096]{1,0:T(8,128)(2,1)S(1)}, bf16[32,4096]{1,0:T(8,128)(2,1)S(1)}, u32[]{:S(2)}, u32[]{:S(2)}) %collective-permute-start.37) | collective-permute-done | bytes 262176 | tf_op jit(solution)/shard_map/ppermute | solution.py:162
  (126 shorter events, 35.4 us)
Async XLA Ops:
  6.4 38.0 %collective-permute-start.1 = (bf16[32,4224]{1,0:T(8,128)(2,1)}, bf16[32,4224]{1,0:T(8,128)(2,1)S(1)}, u32[]{:S(2)}, u32[]{:S(2)}) collective-permute-start(bf16[32,4224]{1,0:T(8,128)(2,1)} %get-tuple-element.8), channel_id=1, source_target_pairs={{0,2},{1,3},{4,0},{5,1},{8,4},{9,5},{12,8},{13,9},{14,12},{15,13},... | collective-permute-start | bytes 811016 | tf_op jit(solution)/shard_map/ppermute | solution.py:165
  9.4 35.0 %collective-permute-start = (bf16[32,4224]{1,0:T(8,128)(2,1)}, bf16[32,4224]{1,0:T(8,128)(2,1)S(1)}, u32[]{:S(2)}, u32[]{:S(2)}) collective-permute-start(bf16[32,4224]{1,0:T(8,128)(2,1)} %get-tuple-element.8), channel_id=1, source_target_pairs={{0,4},{1,5},{4,8},{5,9},{8,12},{9,13},{12,14},{13,15},{14,10},{15,... | collective-permute-start | bytes 811016 | tf_op jit(solution)/shard_map/ppermute | solution.py:162
  13.4 4.6 %copy-start.1 = (bf16[1,4096,1536]{2,1,0:T(8,128)(2,1)S(1)}, bf16[1,4096,1536]{2,1,0:T(8,128)(2,1)}, u32[]{:S(2)}) copy-start(bf16[1,4096,1536]{2,1,0:T(8,128)(2,1)} %param.15) | copy-start | bytes 37748740
  18.0 8.9 %copy-start.2 = (bf16[1,4096,1536]{2,1,0:T(8,128)(2,1)S(1)}, bf16[1,4096,1536]{2,1,0:T(8,128)(2,1)}, u32[]{:S(2)}) copy-start(bf16[1,4096,1536]{2,1,0:T(8,128)(2,1)} %param.14) | copy-start | bytes 37748740
  26.8 19.9 %slice-start = ((s8[4325376]{0:T(1024)(128)(4,1)}), s8[131072]{0:T(1024)(128)(4,1)S(1)}, s32[]{:S(2)}) async-start(s8[4325376]{0:T(1024)(128)(4,1)} %bitcast.15), calls=%async_computation | async-start | bytes 262144
  35.7 4.6 %copy-start = (bf16[1,1536,4096]{2,1,0:T(8,128)(2,1)S(1)}, bf16[1,1536,4096]{2,1,0:T(8,128)(2,1)}, u32[]{:S(2)}) copy-start(bf16[1,1536,4096]{2,1,0:T(8,128)(2,1)} %param.16) | copy-start | bytes 37748740
  40.3 6.5 %slice-start.1 = ((s8[4325376]{0:T(1024)(128)(4,1)}), s8[4194304]{0:T(1024)(128)(4,1)S(1)}, s32[]{:S(2)}) async-start(s8[4325376]{0:T(1024)(128)(4,1)} %bitcast.15), calls=%async_computation.1 | async-start | bytes 8388608
  44.4 21.1 %copy-start.8 = (bf16[32,4224]{1,0:T(8,128)(2,1)S(1)}, bf16[32,4224]{1,0:T(8,128)(2,1)}, u32[]{:S(2)}) copy-start(bf16[32,4224]{1,0:T(8,128)(2,1)} %get-tuple-element.10) | copy-start | bytes 811012
  44.5 38.5 %collective-permute-start.8 = (bf16[96,4224]{1,0:T(8,128)(2,1)S(1)}, bf16[96,4224]{1,0:T(8,128)(2,1)S(1)}, u32[]{:S(2)}, u32[]{:S(2)}) collective-permute-start(bf16[96,4224]{1,0:T(8,128)(2,1)S(1)} %pad_maximum_fusion), channel_id=1, source_target_pairs={{0,1},{1,0},{2,3},{3,2},{4,5},{5,4},{6,7},{7,6},{8,9},{9,8},{10,11... | collective-permute-start | bytes 2433032 | tf_op jit(solution)/shard_map/ppermute | solution.py:168
  44.6 9.1 %collective-permute-start.3 = (bf16[32,4224]{1,0:T(8,128)(2,1)S(1)}, bf16[32,4224]{1,0:T(8,128)(2,1)S(1)}, u32[]{:S(2)}, u32[]{:S(2)}) collective-permute-start(bf16[32,4224]{1,0:T(8,128)(2,1)S(1)} %collective-permute-done.1), channel_id=1, source_target_pairs={{0,2},{1,3},{4,0},{5,1},{8,4},{9,5},{12,8},{13,9},{14,12},{15,13},... | collective-permute-start | bytes 811016 | tf_op jit(solution)/shard_map/ppermute | solution.py:165
  46.6 8.6 %collective-permute-start.2 = (bf16[32,4224]{1,0:T(8,128)(2,1)S(1)}, bf16[32,4224]{1,0:T(8,128)(2,1)S(1)}, u32[]{:S(2)}, u32[]{:S(2)}) collective-permute-start(bf16[32,4224]{1,0:T(8,128)(2,1)S(1)} %collective-permute-done), channel_id=1, source_target_pairs={{0,4},{1,5},{4,8},{5,9},{8,12},{9,13},{12,14},{13,15},{14,10},{15,... | collective-permute-start | bytes 811016 | tf_op jit(solution)/shard_map/ppermute | solution.py:162
  55.2 30.3 %collective-permute-start.9 = (bf16[64,4224]{1,0:T(8,128)(2,1)S(1)}, bf16[64,4224]{1,0:T(8,128)(2,1)S(1)}, u32[]{:S(2)}, u32[]{:S(2)}) collective-permute-start(bf16[64,4224]{1,0:T(8,128)(2,1)S(1)} %pad_maximum_fusion.2), channel_id=1, source_target_pairs={{0,1},{1,0},{2,3},{3,2},{4,5},{5,4},{6,7},{7,6},{8,9},{9,8},{10,11... | collective-permute-start | bytes 1622024 | tf_op jit(solution)/shard_map/ppermute | solution.py:168
  55.3 8.9 %collective-permute-start.5 = (bf16[32,4224]{1,0:T(8,128)(2,1)S(1)}, bf16[32,4224]{1,0:T(8,128)(2,1)S(1)}, u32[]{:S(2)}, u32[]{:S(2)}) collective-permute-start(bf16[32,4224]{1,0:T(8,128)(2,1)S(1)} %collective-permute-done.3), channel_id=1, source_target_pairs={{0,2},{1,3},{4,0},{5,1},{8,4},{9,5},{12,8},{13,9},{14,12},{15,13},... | collective-permute-start | bytes 811016 | tf_op jit(solution)/shard_map/ppermute | solution.py:165
  56.9 8.6 %collective-permute-start.4 = (bf16[32,4224]{1,0:T(8,128)(2,1)S(1)}, bf16[32,4224]{1,0:T(8,128)(2,1)S(1)}, u32[]{:S(2)}, u32[]{:S(2)}) collective-permute-start(bf16[32,4224]{1,0:T(8,128)(2,1)S(1)} %collective-permute-done.2), channel_id=1, source_target_pairs={{0,4},{1,5},{4,8},{5,9},{8,12},{9,13},{12,14},{13,15},{14,10},{15,... | collective-permute-start | bytes 811016 | tf_op jit(solution)/shard_map/ppermute | solution.py:162
  65.5 11.1 %collective-permute-start.22 = (bf16[32,4224]{1,0:T(8,128)(2,1)S(1)}, bf16[32,4224]{1,0:T(8,128)(2,1)S(1)}, u32[]{:S(2)}, u32[]{:S(2)}) collective-permute-start(bf16[32,4224]{1,0:T(8,128)(2,1)S(1)} %copy-done.8), channel_id=1, source_target_pairs={{0,2},{1,3},{4,0},{5,1},{8,4},{9,5},{12,8},{13,9},{14,12},{15,13},... | collective-permute-start | bytes 811016 | tf_op jit(solution)/shard_map/ppermute | solution.py:165
  67.8 8.3 %collective-permute-start.7 = (bf16[16,4224]{1,0:T(8,128)(2,1)S(1)}, bf16[16,4224]{1,0:T(8,128)(2,1)S(1)}, u32[]{:S(2)}, u32[]{:S(2)}) collective-permute-start(bf16[16,4224]{1,0:T(8,128)(2,1)S(1)} %slice.161), channel_id=1, source_target_pairs={{0,2},{1,3},{4,0},{5,1},{8,4},{9,5},{12,8},{13,9},{14,12},{15,13},... | collective-permute-start | bytes 405512 | tf_op jit(solution)/shard_map/ppermute | solution.py:165
  69.4 7.1 %collective-permute-start.6 = (bf16[16,4224]{1,0:T(8,128)(2,1)S(1)}, bf16[16,4224]{1,0:T(8,128)(2,1)S(1)}, u32[]{:S(2)}, u32[]{:S(2)}) collective-permute-start(bf16[16,4224]{1,0:T(8,128)(2,1)S(1)} %slice.160), channel_id=1, source_target_pairs={{0,4},{1,5},{4,8},{5,9},{8,12},{9,13},{12,14},{13,15},{14,10},{15,... | collective-permute-start | bytes 405512 | tf_op jit(solution)/shard_map/ppermute | solution.py:162
  76.1 6.8 %collective-permute-start.21 = (bf16[32,4224]{1,0:T(8,128)(2,1)S(1)}, bf16[32,4224]{1,0:T(8,128)(2,1)S(1)}, u32[]{:S(2)}, u32[]{:S(2)}) collective-permute-start(bf16[32,4224]{1,0:T(8,128)(2,1)S(1)} %copy-done.8), channel_id=1, source_target_pairs={{0,4},{1,5},{4,8},{5,9},{8,12},{9,13},{12,14},{13,15},{14,10},{15,... | collective-permute-start | bytes 811016 | tf_op jit(solution)/shard_map/ppermute | solution.py:162
  76.5 10.2 %collective-permute-start.10 = (bf16[64,4224]{1,0:T(8,128)(2,1)S(1)}, bf16[64,4224]{1,0:T(8,128)(2,1)S(1)}, u32[]{:S(2)}, u32[]{:S(2)}) collective-permute-start(bf16[64,4224]{1,0:T(8,128)(2,1)S(1)} %pad_maximum_fusion.3), channel_id=1, source_target_pairs={{0,1},{1,0},{2,3},{3,2},{4,5},{5,4},{6,7},{7,6},{8,9},{9,8},{10,11... | collective-permute-start | bytes 1622024 | tf_op jit(solution)/shard_map/ppermute | solution.py:168
  76.6 10.2 %collective-permute-start.11 = (bf16[32,4224]{1,0:T(8,128)(2,1)S(1)}, bf16[32,4224]{1,0:T(8,128)(2,1)S(1)}, u32[]{:S(2)}, u32[]{:S(2)}) collective-permute-start(bf16[32,4224]{1,0:T(8,128)(2,1)S(1)} %pad_maximum_fusion.7), channel_id=1, source_target_pairs={{0,1},{1,0},{2,3},{3,2},{4,5},{5,4},{6,7},{7,6},{8,9},{9,8},{10,11... | collective-permute-start | bytes 811016 | tf_op jit(solution)/shard_map/ppermute | solution.py:168
  82.9 46.7 %collective-permute-start.29 = (bf16[96,4224]{1,0:T(8,128)(2,1)S(1)}, bf16[96,4224]{1,0:T(8,128)(2,1)}, u32[]{:S(2)}, u32[]{:S(2)}) collective-permute-start(bf16[96,4224]{1,0:T(8,128)(2,1)S(1)} %pad_maximum_fusion.1), channel_id=1, source_target_pairs={{0,1},{1,0},{2,3},{3,2},{4,5},{5,4},{6,7},{7,6},{8,9},{9,8},{10,11... | collective-permute-start | bytes 2433032 | tf_op jit(solution)/shard_map/ppermute | solution.py:168
  83.0 29.4 %collective-permute-start.24 = (bf16[32,4224]{1,0:T(8,128)(2,1)S(1)}, bf16[32,4224]{1,0:T(8,128)(2,1)S(1)}, u32[]{:S(2)}, u32[]{:S(2)}) collective-permute-start(bf16[32,4224]{1,0:T(8,128)(2,1)S(1)} %collective-permute-done.22), channel_id=1, source_target_pairs={{0,2},{1,3},{4,0},{5,1},{8,4},{9,5},{12,8},{13,9},{14,12},{15,13},... | collective-permute-start | bytes 811016 | tf_op jit(solution)/shard_map/ppermute | solution.py:165
  85.5 27.0 %collective-permute-start.23 = (bf16[32,4224]{1,0:T(8,128)(2,1)S(1)}, bf16[32,4224]{1,0:T(8,128)(2,1)S(1)}, u32[]{:S(2)}, u32[]{:S(2)}) collective-permute-start(bf16[32,4224]{1,0:T(8,128)(2,1)S(1)} %collective-permute-done.21), channel_id=1, source_target_pairs={{0,4},{1,5},{4,8},{5,9},{8,12},{9,13},{12,14},{13,15},{14,10},{15,... | collective-permute-start | bytes 811016 | tf_op jit(solution)/shard_map/ppermute | solution.py:162
  112.4 55.4 %collective-permute-start.12 = (bf16[256,4096]{1,0:T(8,128)(2,1)S(1)}, bf16[256,4096]{1,0:T(8,128)(2,1)S(1)}, u32[]{:S(2)}, u32[]{:S(2)}) collective-permute-start(bf16[256,4096]{1,0:T(8,128)(2,1)S(1)} %down.5), channel_id=1, source_target_pairs={{0,1},{1,0},{2,3},{3,2},{4,5},{5,4},{6,7},{7,6},{8,9},{9,8},{10,11... | collective-permute-start | bytes 6291464 | tf_op jit(solution)/shard_map/ppermute | solution.py:168
  112.5 19.2 %collective-permute-start.30 = (bf16[64,4224]{1,0:T(8,128)(2,1)S(1)}, bf16[64,4224]{1,0:T(8,128)(2,1)S(1)}, u32[]{:S(2)}, u32[]{:S(2)}) collective-permute-start(bf16[64,4224]{1,0:T(8,128)(2,1)S(1)} %pad_maximum_fusion.4), channel_id=1, source_target_pairs={{0,1},{1,0},{2,3},{3,2},{4,5},{5,4},{6,7},{7,6},{8,9},{9,8},{10,11... | collective-permute-start | bytes 1622024 | tf_op jit(solution)/shard_map/ppermute | solution.py:168
  113.1 8.5 %collective-permute-start.26 = (bf16[32,4224]{1,0:T(8,128)(2,1)S(1)}, bf16[32,4224]{1,0:T(8,128)(2,1)S(1)}, u32[]{:S(2)}, u32[]{:S(2)}) collective-permute-start(bf16[32,4224]{1,0:T(8,128)(2,1)S(1)} %collective-permute-done.24), channel_id=1, source_target_pairs={{0,2},{1,3},{4,0},{5,1},{8,4},{9,5},{12,8},{13,9},{14,12},{15,13},... | collective-permute-start | bytes 811016 | tf_op jit(solution)/shard_map/ppermute | solution.py:165
  114.6 8.5 %collective-permute-start.25 = (bf16[32,4224]{1,0:T(8,128)(2,1)S(1)}, bf16[32,4224]{1,0:T(8,128)(2,1)S(1)}, u32[]{:S(2)}, u32[]{:S(2)}) collective-permute-start(bf16[32,4224]{1,0:T(8,128)(2,1)S(1)} %collective-permute-done.23), channel_id=1, source_target_pairs={{0,4},{1,5},{4,8},{5,9},{8,12},{9,13},{12,14},{13,15},{14,10},{15,... | collective-permute-start | bytes 811016 | tf_op jit(solution)/shard_map/ppermute | solution.py:162
  121.5 5.1 %collective-permute-start.28 = (bf16[16,4224]{1,0:T(8,128)(2,1)S(1)}, bf16[16,4224]{1,0:T(8,128)(2,1)S(1)}, u32[]{:S(2)}, u32[]{:S(2)}) collective-permute-start(bf16[16,4224]{1,0:T(8,128)(2,1)S(1)} %slice.181), channel_id=1, source_target_pairs={{0,2},{1,3},{4,0},{5,1},{8,4},{9,5},{12,8},{13,9},{14,12},{15,13},... | collective-permute-start | bytes 405512 | tf_op jit(solution)/shard_map/ppermute | solution.py:165
  123.2 5.1 %collective-permute-start.27 = (bf16[16,4224]{1,0:T(8,128)(2,1)S(1)}, bf16[16,4224]{1,0:T(8,128)(2,1)S(1)}, u32[]{:S(2)}, u32[]{:S(2)}) collective-permute-start(bf16[16,4224]{1,0:T(8,128)(2,1)S(1)} %slice.180), channel_id=1, source_target_pairs={{0,4},{1,5},{4,8},{5,9},{8,12},{9,13},{12,14},{13,15},{14,10},{15,... | collective-permute-start | bytes 405512 | tf_op jit(solution)/shard_map/ppermute | solution.py:162
  126.6 6.0 %collective-permute-start.31 = (bf16[64,4224]{1,0:T(8,128)(2,1)S(1)}, bf16[64,4224]{1,0:T(8,128)(2,1)S(1)}, u32[]{:S(2)}, u32[]{:S(2)}) collective-permute-start(bf16[64,4224]{1,0:T(8,128)(2,1)S(1)} %pad_maximum_fusion.5), channel_id=1, source_target_pairs={{0,1},{1,0},{2,3},{3,2},{4,5},{5,4},{6,7},{7,6},{8,9},{9,8},{10,11... | collective-permute-start | bytes 1622024 | tf_op jit(solution)/shard_map/ppermute | solution.py:168
  128.3 5.3 %collective-permute-start.32 = (bf16[32,4224]{1,0:T(8,128)(2,1)S(1)}, bf16[32,4224]{1,0:T(8,128)(2,1)S(1)}, u32[]{:S(2)}, u32[]{:S(2)}) collective-permute-start(bf16[32,4224]{1,0:T(8,128)(2,1)S(1)} %pad_maximum_fusion.8), channel_id=1, source_target_pairs={{0,1},{1,0},{2,3},{3,2},{4,5},{5,4},{6,7},{7,6},{8,9},{9,8},{10,11... | collective-permute-start | bytes 811016 | tf_op jit(solution)/shard_map/ppermute | solution.py:168
  157.8 12.1 %collective-permute-start.33 = (bf16[256,4096]{1,0:T(8,128)(2,1)S(1)}, bf16[256,4096]{1,0:T(8,128)(2,1)S(1)}, u32[]{:S(2)}, u32[]{:S(2)}) collective-permute-start(bf16[256,4096]{1,0:T(8,128)(2,1)S(1)} %down.7), channel_id=1, source_target_pairs={{0,1},{1,0},{2,3},{3,2},{4,5},{5,4},{6,7},{7,6},{8,9},{9,8},{10,11... | collective-permute-start | bytes 6291464 | tf_op jit(solution)/shard_map/ppermute | solution.py:168
  167.8 6.4 %collective-permute-start.13 = (bf16[16,4096]{1,0:T(8,128)(2,1)S(1)}, bf16[16,4096]{1,0:T(8,128)(2,1)S(1)}, u32[]{:S(2)}, u32[]{:S(2)}) collective-permute-start(bf16[16,4096]{1,0:T(8,128)(2,1)S(1)} %get-tuple-element.17), channel_id=1, source_target_pairs={{0,4},{1,5},{4,8},{5,9},{8,12},{9,13},{12,14},{13,15},{14,10},{15,... | collective-permute-start | bytes 393224 | tf_op jit(solution)/shard_map/ppermute | solution.py:162
  168.3 6.4 %collective-permute-start.17 = (bf16[16,4096]{1,0:T(8,128)(2,1)S(1)}, bf16[16,4096]{1,0:T(8,128)(2,1)S(1)}, u32[]{:S(2)}, u32[]{:S(2)}) collective-permute-start(bf16[16,4096]{1,0:T(8,128)(2,1)S(1)} %get-tuple-element.18), channel_id=1, source_target_pairs={{0,2},{1,3},{4,0},{5,1},{8,4},{9,5},{12,8},{13,9},{14,12},{15,13},... | collective-permute-start | bytes 393224 | tf_op jit(solution)/shard_map/ppermute | solution.py:165
  170.0 7.0 %collective-permute-start.34 = (bf16[16,4096]{1,0:T(8,128)(2,1)S(1)}, bf16[16,4096]{1,0:T(8,128)(2,1)S(1)}, u32[]{:S(2)}, u32[]{:S(2)}) collective-permute-start(bf16[16,4096]{1,0:T(8,128)(2,1)S(1)} %get-tuple-element.25), channel_id=1, source_target_pairs={{0,4},{1,5},{4,8},{5,9},{8,12},{9,13},{12,14},{13,15},{14,10},{15,... | collective-permute-start | bytes 393224 | tf_op jit(solution)/shard_map/ppermute | solution.py:162
  170.5 6.5 %collective-permute-start.38 = (bf16[16,4096]{1,0:T(8,128)(2,1)S(1)}, bf16[16,4096]{1,0:T(8,128)(2,1)S(1)}, u32[]{:S(2)}, u32[]{:S(2)}) collective-permute-start(bf16[16,4096]{1,0:T(8,128)(2,1)S(1)} %get-tuple-element.26), channel_id=1, source_target_pairs={{0,2},{1,3},{4,0},{5,1},{8,4},{9,5},{12,8},{13,9},{14,12},{15,13},... | collective-permute-start | bytes 393224 | tf_op jit(solution)/shard_map/ppermute | solution.py:165
  174.9 9.3 %collective-permute-start.14 = (bf16[32,4096]{1,0:T(8,128)(2,1)S(1)}, bf16[32,4096]{1,0:T(8,128)(2,1)S(1)}, u32[]{:S(2)}, u32[]{:S(2)}) collective-permute-start(bf16[32,4096]{1,0:T(8,128)(2,1)S(1)} %get-tuple-element.15), channel_id=1, source_target_pairs={{0,4},{1,5},{4,8},{5,9},{8,12},{9,13},{12,14},{13,15},{14,10},{15,... | collective-permute-start | bytes 786440 | tf_op jit(solution)/shard_map/ppermute | solution.py:162
  175.4 9.2 %collective-permute-start.18 = (bf16[32,4096]{1,0:T(8,128)(2,1)S(1)}, bf16[32,4096]{1,0:T(8,128)(2,1)S(1)}, u32[]{:S(2)}, u32[]{:S(2)}) collective-permute-start(bf16[32,4096]{1,0:T(8,128)(2,1)S(1)} %get-tuple-element.16), channel_id=1, source_target_pairs={{0,2},{1,3},{4,0},{5,1},{8,4},{9,5},{12,8},{13,9},{14,12},{15,13},... | collective-permute-start | bytes 786440 | tf_op jit(solution)/shard_map/ppermute | solution.py:165
  177.2 12.6 %collective-permute-start.35 = (bf16[32,4096]{1,0:T(8,128)(2,1)S(1)}, bf16[32,4096]{1,0:T(8,128)(2,1)S(1)}, u32[]{:S(2)}, u32[]{:S(2)}) collective-permute-start(bf16[32,4096]{1,0:T(8,128)(2,1)S(1)} %get-tuple-element.23), channel_id=1, source_target_pairs={{0,4},{1,5},{4,8},{5,9},{8,12},{9,13},{12,14},{13,15},{14,10},{15,... | collective-permute-start | bytes 786440 | tf_op jit(solution)/shard_map/ppermute | solution.py:162
  177.6 12.6 %collective-permute-start.39 = (bf16[32,4096]{1,0:T(8,128)(2,1)S(1)}, bf16[32,4096]{1,0:T(8,128)(2,1)S(1)}, u32[]{:S(2)}, u32[]{:S(2)}) collective-permute-start(bf16[32,4096]{1,0:T(8,128)(2,1)S(1)} %get-tuple-element.24), channel_id=1, source_target_pairs={{0,2},{1,3},{4,0},{5,1},{8,4},{9,5},{12,8},{13,9},{14,12},{15,13},... | collective-permute-start | bytes 786440 | tf_op jit(solution)/shard_map/ppermute | solution.py:165
  184.8 10.6 %collective-permute-start.15 = (bf16[32,4096]{1,0:T(8,128)(2,1)S(1)}, bf16[32,4096]{1,0:T(8,128)(2,1)S(1)}, u32[]{:S(2)}, u32[]{:S(2)}) collective-permute-start(bf16[32,4096]{1,0:T(8,128)(2,1)S(1)} %get-tuple-element.13), channel_id=1, source_target_pairs={{0,4},{1,5},{4,8},{5,9},{8,12},{9,13},{12,14},{13,15},{14,10},{15,... | collective-permute-start | bytes 786440 | tf_op jit(solution)/shard_map/ppermute | solution.py:162
  185.9 10.0 %collective-permute-start.19 = (bf16[32,4096]{1,0:T(8,128)(2,1)S(1)}, bf16[32,4096]{1,0:T(8,128)(2,1)S(1)}, u32[]{:S(2)}, u32[]{:S(2)}) collective-permute-start(bf16[32,4096]{1,0:T(8,128)(2,1)S(1)} %get-tuple-element.14), channel_id=1, source_target_pairs={{0,2},{1,3},{4,0},{5,1},{8,4},{9,5},{12,8},{13,9},{14,12},{15,13},... | collective-permute-start | bytes 786440 | tf_op jit(solution)/shard_map/ppermute | solution.py:165
  190.5 10.6 %collective-permute-start.36 = (bf16[32,4096]{1,0:T(8,128)(2,1)S(1)}, bf16[32,4096]{1,0:T(8,128)(2,1)S(1)}, u32[]{:S(2)}, u32[]{:S(2)}) collective-permute-start(bf16[32,4096]{1,0:T(8,128)(2,1)S(1)} %get-tuple-element.21), channel_id=1, source_target_pairs={{0,4},{1,5},{4,8},{5,9},{8,12},{9,13},{12,14},{13,15},{14,10},{15,... | collective-permute-start | bytes 786440 | tf_op jit(solution)/shard_map/ppermute | solution.py:162
  191.5 10.0 %collective-permute-start.40 = (bf16[32,4096]{1,0:T(8,128)(2,1)S(1)}, bf16[32,4096]{1,0:T(8,128)(2,1)S(1)}, u32[]{:S(2)}, u32[]{:S(2)}) collective-permute-start(bf16[32,4096]{1,0:T(8,128)(2,1)S(1)} %get-tuple-element.22), channel_id=1, source_target_pairs={{0,2},{1,3},{4,0},{5,1},{8,4},{9,5},{12,8},{13,9},{14,12},{15,13},... | collective-permute-start | bytes 786440 | tf_op jit(solution)/shard_map/ppermute | solution.py:165
  196.1 10.6 %collective-permute-start.16 = (bf16[32,4096]{1,0:T(8,128)(2,1)S(1)}, bf16[32,4096]{1,0:T(8,128)(2,1)S(1)}, u32[]{:S(2)}, u32[]{:S(2)}) collective-permute-start(bf16[32,4096]{1,0:T(8,128)(2,1)S(1)} %get-tuple-element.11), channel_id=1, source_target_pairs={{0,4},{1,5},{4,8},{5,9},{8,12},{9,13},{12,14},{13,15},{14,10},{15,... | collective-permute-start | bytes 786440 | tf_op jit(solution)/shard_map/ppermute | solution.py:162
  197.1 10.0 %collective-permute-start.20 = (bf16[32,4096]{1,0:T(8,128)(2,1)S(1)}, bf16[32,4096]{1,0:T(8,128)(2,1)S(1)}, u32[]{:S(2)}, u32[]{:S(2)}) collective-permute-start(bf16[32,4096]{1,0:T(8,128)(2,1)S(1)} %get-tuple-element.12), channel_id=1, source_target_pairs={{0,2},{1,3},{4,0},{5,1},{8,4},{9,5},{12,8},{13,9},{14,12},{15,13},... | collective-permute-start | bytes 786440 | tf_op jit(solution)/shard_map/ppermute | solution.py:165
  201.7 8.2 %collective-permute-start.37 = (bf16[32,4096]{1,0:T(8,128)(2,1)S(1)}, bf16[32,4096]{1,0:T(8,128)(2,1)S(1)}, u32[]{:S(2)}, u32[]{:S(2)}) collective-permute-start(bf16[32,4096]{1,0:T(8,128)(2,1)S(1)} %get-tuple-element.19), channel_id=1, source_target_pairs={{0,4},{1,5},{4,8},{5,9},{8,12},{9,13},{12,14},{13,15},{14,10},{15,... | collective-permute-start | bytes 786440 | tf_op jit(solution)/shard_map/ppermute | solution.py:162
  202.8 7.2 %collective-permute-start.41 = (bf16[32,4096]{1,0:T(8,128)(2,1)S(1)}, bf16[32,4096]{1,0:T(8,128)(2,1)S(1)}, u32[]{:S(2)}, u32[]{:S(2)}) collective-permute-start(bf16[32,4096]{1,0:T(8,128)(2,1)S(1)} %get-tuple-element.20), channel_id=1, source_target_pairs={{0,2},{1,3},{4,0},{5,1},{8,4},{9,5},{12,8},{13,9},{14,12},{15,13},... | collective-permute-start | bytes 786440 | tf_op jit(solution)/shard_map/ppermute | solution.py:165
  (6 other events, 19.7 us)
